TPU v7x, 32 devices: a whole 2x2x4 slice. The times are simulated.
32 devices in a mesh: dp: 8 (over z, x), mlp: 4 (over y, core).
Axes of the slice: x: 2, y: 2, z: 4, core: 2. Of those that a mesh axis runs over, the one named last changes fastest.
Arguments:
- tokens: bfloat16 [2, 6304, 768], P(None, ('dp', 'mlp')), may hold values from -6 to 6
- keep_mask: int32 [2, 6304], P(None, ('dp', 'mlp')), may hold values 0 or 1
- position_index: int32 [197, 197], replicated, may hold values from 0 to 731
- cotangent: bfloat16 [2, 6304, 768], P(None, ('dp', 'mlp')), may hold values from -6 to 6
- first_gain: float32 [768], replicated, may hold values from 0.5 to 1.5
- first_shift: float32 [768], replicated, may hold values from -4 to 4
- inner_weight: bfloat16 [768, 2304], P(('dp', 'mlp')), may hold values from -0.21875 to 0.21875
- query_bias: float32 [768], replicated, may hold values from -6 to 6
- value_bias: float32 [768], replicated, may hold values from -6 to 6
- outer_weight: bfloat16 [768, 768], P(('dp', 'mlp')), may hold values from -0.875 to 0.875
- outer_bias: float32 [768], replicated, may hold values from -4 to 4
- attend_scale: float32 [768], replicated, may hold values from 0.5 to 1.5
- second_gain: float32 [768], replicated, may hold values from 0.5 to 1.5
- second_shift: float32 [768], replicated, may hold values from -4 to 4
- up_weight: bfloat16 [768, 3072], P('dp', 'mlp'), may hold values from -0.21875 to 0.21875
- up_bias: float32 [3072], replicated, may hold values from -6 to 6
- down_weight: bfloat16 [3072, 768], P('mlp', 'dp'), may hold values from -0.109375 to 0.109375
- down_bias: float32 [768], replicated, may hold values from -4 to 4
- feed_scale: float32 [768], replicated, may hold values from 0.5 to 1.5
- position_table: float32 [732, 12], replicated, may hold values from -6 to 6
Outputs:
- result: bfloat16 [2, 6304, 768], P(None, ('dp', 'mlp'))
- gradient_tokens: bfloat16 [2, 6304, 768], P(None, ('dp', 'mlp'))
- gradient_inner: float32 [768, 2304], P(('dp', 'mlp'))
- gradient_outer: float32 [768, 768], P(('dp', 'mlp'))
- gradient_up: float32 [768, 3072], P('dp', 'mlp')
- gradient_down: float32 [3072, 768], P('mlp', 'dp')
- gradient_first_gain: float32 [768], replicated
- gradient_first_shift: float32 [768], replicated
- gradient_query_bias: float32 [768], replicated
- gradient_value_bias: float32 [768], replicated
- gradient_outer_bias: float32 [768], replicated
- gradient_attend_scale: float32 [768], replicated
- gradient_second_gain: float32 [768], replicated
- gradient_second_shift: float32 [768], replicated
- gradient_up_bias: float32 [3072], replicated
- gradient_down_bias: float32 [768], replicated
- gradient_feed_scale: float32 [768], replicated
- gradient_table: float32 [732, 12], replicated
All inputs are finite; a program needn't handle non-finite values. No bound on the sum of `keep_mask` on one device may be relied on, other than what follows from the above.
Results may differ from a plain program's by a relative error of at most 0.014.
Values may be sent and summed in bfloat16 or wider, within the bound.
A program may use at most 192 MiB of HBM per device.

v0:
```python
import jax
import jax.numpy as jnp
from jax import lax
from jax.sharding import PartitionSpec as P

EPS = 1e-06
ROOT_HALF = 0.7071067811865476
DENSITY = 0.3989422804014327


def layer_norm(values, gain, shift):
    mean = jnp.mean(values, -1, keepdims=True)
    centred = values - mean
    variance = jnp.mean(centred * centred, -1, keepdims=True)
    scaled = lax.rsqrt(variance + EPS)
    unit = centred * scaled
    return (unit * gain + shift, unit, scaled)


def norm_back(upstream, unit, scaled, gain):
    inner = upstream * gain
    first = jnp.mean(inner, -1, keepdims=True)
    second = jnp.mean(inner * unit, -1, keepdims=True)
    return (
        scaled * (inner - first - unit * second),
        jnp.sum(upstream * unit, 0),
        jnp.sum(upstream, 0),
    )


def gelu_pair(pre):
    cumul = 0.5 * (1.0 + lax.erf(pre * ROOT_HALF))
    return (pre * cumul, cumul + pre * jnp.exp(-0.5 * pre * pre) * DENSITY)


def fetch(inner_weight, outer_weight, up_weight, down_weight):
    inner_full, outer_full = (
        lax.all_gather(inner_weight, ("dp", "mlp"), axis=0, tiled=True),
        lax.all_gather(outer_weight, ("dp", "mlp"), axis=0, tiled=True),
    )
    up_full, down_full = (
        lax.all_gather(up_weight, "dp", axis=0, tiled=True),
        lax.all_gather(down_weight, "dp", axis=1, tiled=True),
    )
    return (inner_full, outer_full, up_full, down_full)


def contract_rows(left, right):
    return lax.dot_general(
        left, right, (((0,), (0,)), ((), ())), preferred_element_type=jnp.float32
    )


def contract_cols(left, right):
    return lax.dot_general(
        left, right, (((1,), (1,)), ((), ())), preferred_element_type=jnp.float32
    )


def logits_of(query, keys, bias, allowed, factor):
    raw = jnp.einsum("qhd,khd->hqk", query, keys, preferred_element_type=jnp.float32) * factor
    return jnp.where(allowed, raw + bias, -1e30)


def body(
    tokens,
    keep_mask,
    position_index,
    cotangent,
    first_gain,
    first_shift,
    inner_weight,
    query_bias,
    value_bias,
    outer_weight,
    outer_bias,
    attend_scale,
    second_gain,
    second_shift,
    up_weight,
    up_bias,
    down_weight,
    down_bias,
    feed_scale,
    position_table,
):
    micro, rows, width = tokens.shape
    heads = position_table.shape[1]
    head_dim = width // heads
    factor = head_dim ** (-0.5)
    entries = position_table.shape[0]
    columns = up_weight.shape[1]
    col_start = lax.axis_index("mlp") * columns
    up_local = lax.dynamic_slice_in_dim(up_bias, col_start, columns, 0)
    shift_vector = jnp.concatenate([query_bias, jnp.zeros_like(query_bias), value_bias])
    table_by_head = jnp.transpose(position_table)
    bias = table_by_head[:, position_index]
    seen = jnp.arange(rows)
    diagonal = seen[:, None] == seen[None, :]
    flat_index = position_index.reshape(rows * rows)
    zero_width = jnp.zeros((width,), jnp.float32)
    sum_inner = jnp.zeros((width, 3 * width), jnp.float32)
    sum_outer = jnp.zeros((width, width), jnp.float32)
    sum_up = jnp.zeros((width, columns), jnp.float32)
    sum_down = jnp.zeros((columns, width), jnp.float32)
    sum_table_heads = jnp.zeros((heads, entries), jnp.float32)
    sum_up_bias = jnp.zeros((columns,), jnp.float32)
    sum_first_gain = zero_width
    sum_first_shift = zero_width
    sum_query_bias = zero_width
    sum_value_bias = zero_width
    sum_outer_bias = zero_width
    sum_attend_scale = zero_width
    sum_second_gain = zero_width
    sum_second_shift = zero_width
    sum_down_bias = zero_width
    sum_feed_scale = zero_width
    results = []
    input_grads = []
    for index in range(micro):
        inner_full, outer_full, up_full, down_full = fetch(
            inner_weight, outer_weight, up_weight, down_weight
        )
        source = tokens[index].astype(jnp.float32)
        allowed = jnp.logical_or(keep_mask[index][None, :] == 1, diagonal)[None]
        normed_one, unit_one, scaled_one = layer_norm(source, first_gain, first_shift)
        normed_one = normed_one.astype(jnp.bfloat16)
        projected = (
            jnp.dot(normed_one, inner_full, preferred_element_type=jnp.float32) + shift_vector
        ).astype(jnp.bfloat16)
        query = projected[:, :width].reshape(rows, heads, head_dim)
        keys = projected[:, width : 2 * width].reshape(rows, heads, head_dim)
        values = projected[:, 2 * width :].reshape(rows, heads, head_dim)
        logits = logits_of(query, keys, bias, allowed, factor)
        top = jnp.max(logits, -1, keepdims=True)
        expd = jnp.exp(logits - top)
        total = jnp.sum(expd, -1, keepdims=True)
        probs = expd / total
        log_total = top + jnp.log(total)
        mixed = jnp.einsum(
            "hqk,khd->qhd", probs.astype(jnp.bfloat16), values, preferred_element_type=jnp.float32
        )
        mixed = mixed.reshape(rows, width).astype(jnp.bfloat16)
        attend = jnp.dot(mixed, outer_full, preferred_element_type=jnp.float32) + outer_bias
        resid = source + attend_scale * attend
        normed_two, unit_two, scaled_two = layer_norm(resid, second_gain, second_shift)
        normed_two = normed_two.astype(jnp.bfloat16)
        sequence_rows = lax.all_gather(normed_two, "mlp", axis=0, tiled=True)
        pre = jnp.dot(sequence_rows, up_full, preferred_element_type=jnp.float32) + up_local
        active, slope = gelu_pair(pre)
        hidden = active.astype(jnp.bfloat16)
        feed = (
            lax.psum_scatter(
                jnp.dot(hidden, down_full, preferred_element_type=jnp.float32).astype(jnp.bfloat16),
                "mlp",
                scatter_dimension=0,
                tiled=True,
            ).astype(jnp.float32)
            + down_bias
        )
        results.append((resid + feed_scale * feed).astype(jnp.bfloat16))
        inner_full, outer_full, up_full, down_full = fetch(
            inner_weight, outer_weight, up_weight, down_weight
        )
        upstream = cotangent[index].astype(jnp.float32)
        sum_feed_scale = sum_feed_scale + jnp.sum(feed * upstream, 0)
        dfeed = feed_scale * upstream
        sum_down_bias = sum_down_bias + jnp.sum(dfeed, 0)
        upstream_all = lax.all_gather(dfeed.astype(jnp.bfloat16), "mlp", axis=0, tiled=True)
        sum_down = sum_down + contract_rows(hidden, upstream_all)
        dpre = (contract_cols(upstream_all, down_full) * slope).astype(jnp.bfloat16)
        sum_up_bias = sum_up_bias + jnp.sum(dpre.astype(jnp.float32), 0)
        sum_up = sum_up + contract_rows(sequence_rows, dpre)
        dnormed_two = lax.psum_scatter(
            contract_cols(dpre, up_full).astype(jnp.bfloat16),
            "mlp",
            scatter_dimension=0,
            tiled=True,
        ).astype(jnp.float32)
        dresid_norm, part_gain, part_shift = norm_back(
            dnormed_two, unit_two, scaled_two, second_gain
        )
        sum_second_gain = sum_second_gain + part_gain
        sum_second_shift = sum_second_shift + part_shift
        dresid = upstream + dresid_norm
        sum_attend_scale = sum_attend_scale + jnp.sum(attend * dresid, 0)
        dattend = attend_scale * dresid
        sum_outer_bias = sum_outer_bias + jnp.sum(dattend, 0)
        dattend_low = dattend.astype(jnp.bfloat16)
        sum_outer = sum_outer + contract_rows(mixed, dattend_low)
        dmixed = (
            contract_cols(dattend_low, outer_full)
            .astype(jnp.bfloat16)
            .reshape(rows, heads, head_dim)
        )
        logits = logits_of(query, keys, bias, allowed, factor)
        probs = jnp.exp(logits - log_total)
        dvalues = jnp.einsum(
            "hqk,qhd->khd", probs.astype(jnp.bfloat16), dmixed, preferred_element_type=jnp.float32
        )
        dprobs = jnp.einsum("qhd,khd->hqk", dmixed, values, preferred_element_type=jnp.float32)
        dlogits = probs * (dprobs - jnp.sum(dprobs * probs, -1, keepdims=True))
        sum_table_heads = sum_table_heads.at[:, flat_index].add(dlogits.reshape(heads, rows * rows))
        dlogits_low = dlogits.astype(jnp.bfloat16)
        dquery = (
            jnp.einsum("hqk,khd->qhd", dlogits_low, keys, preferred_element_type=jnp.float32)
            * factor
        )
        dkeys = (
            jnp.einsum("hqk,qhd->khd", dlogits_low, query, preferred_element_type=jnp.float32)
            * factor
        )
        dprojected = jnp.concatenate(
            [dquery.reshape(rows, width), dkeys.reshape(rows, width), dvalues.reshape(rows, width)],
            axis=1,
        ).astype(jnp.bfloat16)
        sum_query_bias = sum_query_bias + jnp.sum(dprojected[:, :width].astype(jnp.float32), 0)
        sum_value_bias = sum_value_bias + jnp.sum(dprojected[:, 2 * width :].astype(jnp.float32), 0)
        sum_inner = sum_inner + contract_rows(normed_one, dprojected)
        dnormed_one = contract_cols(dprojected, inner_full)
        dsource_norm, part_gain, part_shift = norm_back(
            dnormed_one, unit_one, scaled_one, first_gain
        )
        sum_first_gain = sum_first_gain + part_gain
        sum_first_shift = sum_first_shift + part_shift
        input_grads.append((dresid + dsource_norm).astype(jnp.bfloat16))
    sum_table = jnp.transpose(sum_table_heads)
    gradient_inner, gradient_outer = (
        lax.psum_scatter(sum_inner, ("dp", "mlp"), scatter_dimension=0, tiled=True),
        lax.psum_scatter(sum_outer, ("dp", "mlp"), scatter_dimension=0, tiled=True),
    )
    gradient_up, gradient_down = (
        lax.psum_scatter(sum_up, "dp", scatter_dimension=0, tiled=True),
        lax.psum_scatter(sum_down, "dp", scatter_dimension=1, tiled=True),
    )
    up_bias_full = lax.dynamic_update_slice_in_dim(
        jnp.zeros((up_bias.shape[0],), jnp.float32), sum_up_bias, col_start, 0
    )
    summed = lax.psum(
        (
            sum_first_gain,
            sum_first_shift,
            sum_query_bias,
            sum_value_bias,
            sum_outer_bias,
            sum_attend_scale,
            sum_second_gain,
            sum_second_shift,
            up_bias_full,
            sum_down_bias,
            sum_feed_scale,
            sum_table,
        ),
        ("dp", "mlp"),
    )
    return (
        jnp.stack(results),
        jnp.stack(input_grads),
        gradient_inner,
        gradient_outer,
        gradient_up,
        gradient_down,
        summed[0],
        summed[1],
        summed[2],
        summed[3],
        summed[4],
        summed[5],
        summed[6],
        summed[7],
        summed[8],
        summed[9],
        summed[10],
        summed[11],
    )


def solution(mesh):
    placed = (
        P(None, ("dp", "mlp"), None),
        P(None, ("dp", "mlp")),
        P(),
        P(None, ("dp", "mlp"), None),
        P(),
        P(),
        P(("dp", "mlp"), None),
        P(),
        P(),
        P(("dp", "mlp"), None),
        P(),
        P(),
        P(),
        P(),
        P("dp", "mlp"),
        P(),
        P("mlp", "dp"),
        P(),
        P(),
        P(),
    )
    return jax.shard_map(
        body,
        mesh=mesh,
        in_specs=placed,
        out_specs=(
            P(None, ("dp", "mlp"), None),
            P(None, ("dp", "mlp"), None),
            P(("dp", "mlp"), None),
            P(("dp", "mlp"), None),
            P("dp", "mlp"),
            P("mlp", "dp"),
            P(),
            P(),
            P(),
            P(),
            P(),
            P(),
            P(),
            P(),
            P(),
            P(),
            P(),
            P(),
        ),
        check_vma=False,
    )
```

profile of v0, /device:TPU:0, one launch (start us, length us, event | category | flops | bytes accessed | tf_op | source)
XLA Modules:
  0.0 1434.0 jit_solution(9241634660880689768)
XLA Ops:
  8.7 2.4 fusion.121
  14.9 128.7 %gather_fusion = f32[38809,12]{1,0:T(8,128)} fusion(f32[12,732]{0,1:T(8,128)S(1)} %bitcast.219, s32[38912]{0:T(1024)S(1)} %pad_clamp_fusion), kind=kCustom, calls=%fused_computation | custom fusion | bytes 3880900 | tf_op jit(solution)/shard_map/gather | solution.py:97
  143.5 11.1 copy.105
  154.6 2.8 reshape.322
  157.4 2.3 copy.106
  160.3 3.3 fusion.5
  164.5 1.9 copy.109
  166.4 1.9 copy.110
  168.3 1.9 copy.111
  170.2 3.0 fusion.4
  176.2 2.0 copy.103
  186.5 1.9 convolution_add_fusion.6
  199.2 2.7 reshape.350
  201.9 2.7 reshape.348
  204.7 7.7 all-gather.23.cloned.1.call-done
  212.4 2.6 reshape.346
  215.0 16.5 %all-gather.21.cloned.1.call-done = bf16[4,197,768]{2,1,0:T(8,128)(2,1)} async-done(((bf16[1,197,768]{2,1,0:T(8,128)(2,1)}), bf16[4,197,768]{2,1,0:T(8,128)(2,1)}) %all-gather.21.cloned.1.call-update) | async-done | bytes 1210384 | tf_op jit(solution)/shard_map/all_gather | solution.py:148
  231.6 2.6 reshape.344
  234.2 40.6 %all-gather.17.cloned.1.call-done = bf16[768,768]{1,0:T(8,128)(2,1)} async-done(((bf16[96,768]{1,0:T(8,128)(2,1)}), bf16[768,768]{1,0:T(8,128)(2,1)}) %all-gather.17.cloned.1.call-update) | async-done | bytes 1179664 | tf_op jit(solution)/shard_map/all_gather | solution.py:42
  274.9 2.9 fusion.125
  279.2 3.5 multiply_convert_fusion.1
  282.8 34.1 %all-gather.19.cloned.1.call-done = bf16[768,768]{0,1:T(8,128)(2,1)} async-done(((bf16[768,96]{0,1:T(8,128)(2,1)}), bf16[768,768]{0,1:T(8,128)(2,1)}) %all-gather.19.cloned.1.call-update) | async-done | bytes 1179664 | tf_op jit(solution)/shard_map/all_gather | solution.py:43
  316.9 4.0 convolution_convert_fusion.2
  320.9 2.3 convolution_convert_fusion.3
  323.2 2.3 convert_reduce_fusion
  325.5 2.2 convolution_convert_fusion
  328.4 2.2 convert_reduce_fusion.1
  331.7 2.2 convolution_convert_fusion.1
  333.9 46.6 %fusion.114 = (bf16[200,768]{1,0:T(8,128)(2,1)}, bf16[200,768]{1,0:T(8,128)(2,1)}, bf16[200,768]{1,0:T(8,128)(2,1)}, bf16[200,768]{1,0:T(8,128)(2,1)}) fusion(bf16[788,768]{1,0:T(8,128)(2,1)} %convolution_convert_fusion.2, bf16[788,768]{1,0:T(8,128)(2,1)} %convolution_convert_fusion.3, bf16[788,768]{1,0:T(8,128)(2,1)} %convolution_convert_fusion, ...), kind=kCustom, calls=%all-reduce-scatter.4 | all-reduce-scatter fusion | flops 2457601 | bytes 6070784
  381.3 1.9 collective-permute-start.2
  383.9 3.2 collective-permute-start.1
  387.9 1.9 collective-permute-start.3
  390.6 1.9 collective-permute-start
  393.0 4.0 concatenate.17
  399.7 4.0 concatenate.16
  403.7 4.0 concatenate.15
  407.8 3.4 fusion.82
  413.3 1.9 copy.119
  415.2 3.2 convolution_convert_fusion.4
  422.9 4.0 concatenate.14
  426.9 3.0 multiply_reduce_fusion.3
  438.9 1.9 fusion.105
  440.8 3.4 copy.123
  444.2 2.2 copy.125
  448.8 4.7 fusion.74
  453.9 2.9 reshape.326
  456.8 9.7 copy.124
  466.6 2.8 reshape.334
  469.3 9.7 copy.126
  479.0 3.8 fusion.90
  490.0 207.4 %scatter_custom_fusion = f32[12,732]{0,1:T(8,128)S(1)} fusion(s32[38809]{0:T(1024)S(1)} %bitcast.254, f32[38809,12]{1,0:T(8,128)} %copy.124, f32[]{:T(128)} %constant.17.clone.1), kind=kCustom, calls=%fused_computation.189 | custom fusion | flops 465708 | bytes 35648 | tf_op jit(solution)/shard_map/scatter-add | solution.py:203
  697.5 207.6 %scatter_fusion = f32[12,732]{0,1:T(8,128)S(1)} fusion(f32[12,732]{0,1:T(8,128)S(1)} %scatter_custom_fusion, s32[38809]{0:T(1024)S(1)} %bitcast.255, f32[38809,12]{1,0:T(8,128)} %copy.126), kind=kCustom, calls=%fused_computation.2 | custom fusion | flops 465708 | bytes 5743732 | tf_op jit(solution)/shard_map/scatter-add | solution.py:203
  905.9 3.6 convolution_add_fusion.3
  909.8 3.2 fusion.126
  913.1 3.0 convolution_add_fusion.5
  916.2 3.3 fusion.127
  919.5 2.9 convolution_add_fusion.4
  923.6 2.4 fusion.91
  926.0 4.3 convolution_add_fusion
  934.3 102.6 %all-reduce.12.cloned.1.call-done = (f32[768]{0:T(1024)}, f32[768]{0:T(1024)}, f32[768]{0:T(1024)}, f32[768]{0:T(1024)}, f32[768]{0:T(1024)}, /*index=5*/f32[768...) async-done(((f32[768]{0:T(1024)}, f32[768]{0:T(1024)}, f32[768]{0:T(1024)}, ...) | async-done | bytes 78160 | tf_op jit(solution)/shard_map/psum | solution.py:239
  1038.7 104.1 %reduce-scatter.15.cloned.1.call-done = f32[24,768]{1,0:T(8,128)} async-done(((f32[768,768]{1,0:T(8,128)}), f32[24,768]{1,0:T(8,128)}) %reduce-scatter.15.cloned.1.call-update) | async-done | bytes 73744 | tf_op jit(solution)/shard_map/reduce_scatter | solution.py:230
  1142.8 72.6 %reduce-scatter.17.cloned.1.call-done = f32[96,768]{1,0:T(8,128)} async-done(((f32[768,768]{1,0:T(8,128)}), f32[96,768]{1,0:T(8,128)}) %reduce-scatter.17.cloned.1.call-update) | async-done | bytes 294928 | tf_op jit(solution)/shard_map/reduce_scatter | solution.py:233
  1215.4 72.4 %reduce-scatter.19.cloned.1.call-done = f32[768,96]{0,1:T(8,128)} async-done(((f32[768,768]{0,1:T(8,128)}), f32[768,96]{0,1:T(8,128)}) %reduce-scatter.19.cloned.1.call-update) | async-done | bytes 294928 | tf_op jit(solution)/shard_map/reduce_scatter | solution.py:234
  1287.8 125.4 %reduce-scatter.13.cloned.1.call-done = f32[24,2304]{1,0:T(8,128)} async-done(((f32[768,2304]{1,0:T(8,128)}), f32[24,2304]{1,0:T(8,128)}) %reduce-scatter.13.cloned.1.call-update) | async-done | bytes 221200 | tf_op jit(solution)/shard_map/reduce_scatter | solution.py:229
  (344 shorter events, 84.4 us)
Async XLA Ops:
  7.2 3.9 copy-start.70
  7.2 153.0 %all-gather.13.cloned.1.call-start = ((), (), s32[]{:S(2)}) async-start(), calls=%async_computation.4 | async-start | bytes 3649536 | tf_op jit(solution)/shard_map/all_gather | solution.py:38
  7.9 178.5 %all-gather.15.cloned.1.call-start = ((), (), s32[]{:S(2)}) async-start(), calls=%async_computation.5 | async-start | bytes 1216512 | tf_op jit(solution)/shard_map/all_gather | solution.py:39
  8.7 4.3 copy-start.36
  8.7 190.5 %all-gather.27.cloned.1.call-start = ((), (), s32[]{:S(2)}) async-start(), calls=%async_computation.15 | async-start | bytes 1536000 | tf_op jit(solution)/shard_map/all_gather | solution.py:169
  12.3 189.6 %all-gather.25.cloned.1.call-start = ((), (), s32[]{:S(2)}) async-start(), calls=%async_computation.14 | async-start | bytes 1536000 | tf_op jit(solution)/shard_map/all_gather | solution.py:169
  12.9 199.5 %all-gather.23.cloned.1.call-start = ((), (), s32[]{:S(2)}) async-start(), calls=%async_computation.13 | async-start | bytes 1536000 | tf_op jit(solution)/shard_map/all_gather | solution.py:148
  14.0 156.2 %copy-start.17 = (bf16[1,197,768]{2,1,0:T(8,128)(2,1)}, bf16[1,197,768]{2,1,0:T(8,128)(2,1)S(1)}, u32[]{:S(2)}) copy-start(bf16[1,197,768]{2,1,0:T(8,128)(2,1)S(1)} %get-tuple-element.179) | copy-start | bytes 907780
  14.3 146.0 %copy-start.72 = (f32[197]{0:T(256)}, f32[197]{0:T(256)S(1)}, u32[]{:S(2)}) copy-start(f32[197]{0:T(256)S(1)} %add_rsqrt_fusion.1) | copy-start | bytes 2368
  159.7 18.5 %copy-start.6 = (f32[197,197,12]{0,1,2:T(8,128)}, f32[197,197,12]{0,1,2:T(8,128)S(1)}, u32[]{:S(2)}) copy-start(f32[197,197,12]{0,1,2:T(8,128)S(1)} %copy.106) | copy-start | bytes 5588500
  159.8 10.4 copy-start.78
  160.0 10.2 copy-start.88
  176.2 6.6 copy-start.24
  185.1 3.4 copy-start.58
  189.9 4.0 copy-start.74
  190.1 3.8 copy-start.76
  190.4 3.6 copy-start.83
  191.8 39.7 %all-gather.21.cloned.1.call-start = ((), (), s32[]{:S(2)}) async-start(), calls=%async_computation.12 | async-start | bytes 1536000 | tf_op jit(solution)/shard_map/all_gather | solution.py:148
  192.4 82.4 %all-gather.17.cloned.1.call-start = ((), (), s32[]{:S(2)}) async-start(), calls=%async_computation.6 | async-start | bytes 1327104 | tf_op jit(solution)/shard_map/all_gather | solution.py:42
  193.2 123.7 %all-gather.19.cloned.1.call-start = ((), (), s32[]{:S(2)}) async-start(), calls=%async_computation.7 | async-start | bytes 1327104 | tf_op jit(solution)/shard_map/all_gather | solution.py:43
  194.0 842.9 %all-reduce.12.cloned.1.call-start = ((), (), s32[]{:S(2)}) async-start(), calls=%async_computation.16 | async-start | bytes 860160 | tf_op jit(solution)/shard_map/psum | solution.py:239
  199.1 5.5 copy-start.60
  199.1 5.5 copy-start.64
  199.1 5.5 copy-start.62
  199.2 5.5 copy-start.66
  274.8 4.4 copy-start.52
  274.9 4.4 copy-start.94
  316.9 4.0 copy-start.96
  316.9 4.0 copy-start.101
  333.9 63.1 %copy-start.77 = (f32[197]{0:T(256)S(1)}, f32[197]{0:T(256)}, u32[]{:S(2)}) copy-start(f32[197]{0:T(256)} %copy-done.76) | copy-start | bytes 2368
  333.9 63.1 %copy-start.87 = (f32[197]{0:T(256)S(1)}, f32[197]{0:T(256)}, u32[]{:S(2)}) copy-start(f32[197]{0:T(256)} %copy-done.86) | copy-start | bytes 2368
  380.5 27.3 %copy-start.71 = (f32[768]{0:T(1024)S(1)}, f32[768]{0:T(1024)}, u32[]{:S(2)}) copy-start(f32[768]{0:T(1024)} %param.38) | copy-start | bytes 9220
  380.5 27.3 %copy-start.75 = (f32[197]{0:T(256)S(1)}, f32[197]{0:T(256)}, u32[]{:S(2)}) copy-start(f32[197]{0:T(256)} %copy-done.74) | copy-start | bytes 2368
  380.5 27.3 %copy-start.81 = (f32[768]{0:T(1024)S(1)}, f32[768]{0:T(1024)}, u32[]{:S(2)}) copy-start(f32[768]{0:T(1024)} %param.37) | copy-start | bytes 9220
  380.5 27.3 %copy-start.84 = (f32[197]{0:T(256)S(1)}, f32[197]{0:T(256)}, u32[]{:S(2)}) copy-start(f32[197]{0:T(256)} %copy-done.83) | copy-start | bytes 2368
  381.3 18.4 %collective-permute-start.2 = (bf16[9,768]{1,0:T(8,128)(2,1)S(1)}, bf16[9,768]{1,0:T(8,128)(2,1)}, u32[]{:S(2)}, u32[]{:S(2)}) collective-permute-start(bf16[9,768]{1,0:T(8,128)(2,1)S(1)} %slice.62), channel_id=1, source_target_pairs={{0,1},{1,2},{2,3},{4,5},{5,6},{6,7},{8,9},{9,10},{10,11},{12,13},{... | collective-permute-start | bytes 41480
  383.9 19.8 %collective-permute-start.1 = (bf16[9,768]{1,0:T(8,128)(2,1)S(1)}, bf16[9,768]{1,0:T(8,128)(2,1)}, u32[]{:S(2)}, u32[]{:S(2)}) collective-permute-start(bf16[9,768]{1,0:T(8,128)(2,1)S(1)} %slice.61), channel_id=1, source_target_pairs={{0,1},{1,2},{2,3},{4,5},{5,6},{6,7},{8,9},{9,10},{10,11},{12,13},{... | collective-permute-start | bytes 41480
  387.9 5.1 collective-permute-start.3
  390.6 32.3 %collective-permute-start = (bf16[9,768]{1,0:T(8,128)(2,1)S(1)}, bf16[9,768]{1,0:T(8,128)(2,1)}, u32[]{:S(2)}, u32[]{:S(2)}) collective-permute-start(bf16[9,768]{1,0:T(8,128)(2,1)S(1)} %slice.60), channel_id=1, source_target_pairs={{0,1},{1,2},{2,3},{4,5},{5,6},{6,7},{8,9},{9,10},{10,11},{12,13},{... | collective-permute-start | bytes 41480
  393.0 18.2 %copy-start.69 = (f32[3072]{0:T(1024)}, f32[3072]{0:T(1024)S(1)}, u32[]{:S(2)}) copy-start(f32[3072]{0:T(1024)S(1)} %add_dynamic-update-slice_fusion) | copy-start | bytes 36868
  407.7 4.3 copy-start.9
  421.7 5.2 copy-start.82
  421.7 5.2 copy-start.85
  426.9 3.8 copy-start.10
  440.8 3.4 copy-start.4
  444.2 4.5 copy-start.19
  444.2 4.5 copy-start.79
  444.2 4.5 copy-start.89
  448.8 4.7 copy-start.32
  448.8 4.9 copy-start.30
  479.0 3.8 copy-start.14
  479.0 3.8 copy-start.55
  479.0 3.8 copy-start.73
  482.8 7.3 copy-start.34
  482.8 7.3 copy-start.54
  697.5 208.5 %copy-start.16 = (f32[197,768]{1,0:T(8,128)S(1)}, f32[197,768]{1,0:T(8,128)}, u32[]{:S(2)}) copy-start(f32[197,768]{1,0:T(8,128)} %copy-done.15) | copy-start | bytes 1815556
  697.5 208.5 %copy-start.43 = (bf16[12,64,197]{2,1,0:T(8,128)(2,1)S(1)}, bf16[12,64,197]{2,1,0:T(8,128)(2,1)}, u32[]{:S(2)}) copy-start(bf16[12,64,197]{2,1,0:T(8,128)(2,1)} %convolution_convert_fusion.6) | copy-start | bytes 907780
  905.9 236.9 %reduce-scatter.15.cloned.1.call-start = ((), (), s32[]{:S(2)}) async-start(), calls=%async_computation.9 | async-start | bytes 2433024 | tf_op jit(solution)/shard_map/reduce_scatter | solution.py:230
  909.5 3.5 copy-start.51
  909.5 305.9 %reduce-scatter.17.cloned.1.call-start = ((), (), s32[]{:S(2)}) async-start(), calls=%async_computation.10 | async-start | bytes 2654208 | tf_op jit(solution)/shard_map/reduce_scatter | solution.py:233
  916.1 3.4 copy-start.49
  916.1 371.7 %reduce-scatter.19.cloned.1.call-start = ((), (), s32[]{:S(2)}) async-start(), calls=%async_computation.11 | async-start | bytes 2654208 | tf_op jit(solution)/shard_map/reduce_scatter | solution.py:234
  922.5 3.5 copy-start.31
  922.5 490.8 %reduce-scatter.13.cloned.1.call-start = ((), (), s32[]{:S(2)}) async-start(), calls=%async_computation.8 | async-start | bytes 7299072 | tf_op jit(solution)/shard_map/reduce_scatter | solution.py:229
  (58 other events, 115.9 us)
Sparse Core Ops, SparseCore 0:
  10.9 62.8 all-gather.12
  76.7 52.8 all-gather.14
  131.2 16.6 all-gather.26
  149.3 17.7 all-gather.24
  192.0 20.3 all-gather.22
  213.8 17.7 all-gather.20
  233.8 41.0 all-gather.16
  277.0 39.8 all-gather.18
  906.0 130.8 all-reduce.11
  1042.6 100.1 reduce-scatter.14
  1147.3 68.0 reduce-scatter.16
  1219.7 68.0 reduce-scatter.18
  1295.0 118.1 reduce-scatter.12
where the time goes:
time: 1440 us; the launch traced here: 1430 us
  waiting for transfers between devices  580 us (40%)
  other arithmetic  441 us (31%)
  local copies, waits for them, and re-layouts  257 us (18%)
  matrix products  83.5 us (6%)
  blocking collectives  46.6 us (3%)
  between operations  16.1 us (1%)
    scatter-add x2, other arithmetic, body(): sum_table_heads.at[:, flat_index].add(dlogits.reshape(heads, rows * rows))  415 us
    gather x4, local copies, waits for them, and re-layouts, body(): bias = table_by_head[:, position_index]  145 us
    reduce_scatter x1, waiting for transfers between devices, body(): lax.psum_scatter(sum_inner, ('dp', 'mlp'), scatter_dimension=0, tiled=True)  125 us
    reduce_scatter x1, waiting for transfers between devices, body(): lax.psum_scatter(sum_outer, ('dp', 'mlp'), scatter_dimension=0, tiled=True)  104 us
    psum x1, waiting for transfers between devices, body(): lax.psum((sum_first_gain, sum_first_shift, sum_query_bias, sum_value_bias...  103 us
    reduce_scatter x1, waiting for transfers between devices, body(): lax.psum_scatter(sum_up, 'dp', scatter_dimension=0, tiled=True)  72.6 us
    reduce_scatter x1, waiting for transfers between devices, body(): lax.psum_scatter(sum_down, 'dp', scatter_dimension=1, tiled=True)  72.4 us
    unnamed x238, local copies, waits for them, and re-layouts  60.9 us
  transfers between devices with their start and end apart: 17, of which 9 were waited for; matrix products, arithmetic and copies ran while one was open for 18% of the time, Pallas kernels for 0%

commit v1 on v0

--- a/solution.py
+++ b/solution.py
@@ -2,6 +2,7 @@
 import jax.numpy as jnp
 from jax import lax
 from jax.sharding import PartitionSpec as P
+from jax.lax import psum
 
 EPS = 1e-06
 ROOT_HALF = 0.7071067811865476
@@ -236,22 +237,25 @@
     up_bias_full = lax.dynamic_update_slice_in_dim(
         jnp.zeros((up_bias.shape[0],), jnp.float32), sum_up_bias, col_start, 0
     )
-    summed = lax.psum(
-        (
-            sum_first_gain,
-            sum_first_shift,
-            sum_query_bias,
-            sum_value_bias,
-            sum_outer_bias,
-            sum_attend_scale,
-            sum_second_gain,
-            sum_second_shift,
-            up_bias_full,
-            sum_down_bias,
-            sum_feed_scale,
-            sum_table,
+    summed = psum(
+        psum(
+            (
+                sum_first_gain,
+                sum_first_shift,
+                sum_query_bias,
+                sum_value_bias,
+                sum_outer_bias,
+                sum_attend_scale,
+                sum_second_gain,
+                sum_second_shift,
+                up_bias_full,
+                sum_down_bias,
+                sum_feed_scale,
+                sum_table,
+            ),
+            axis_name="mlp",
         ),
-        ("dp", "mlp"),
+        "dp",
     )
     return (
         jnp.stack(results),

time: 1440 us -> 1420 us (0.986)
  waiting for transfers between devices: 580 us -> 559 us
    psum x1 -> x2, waiting for transfers between devices: 103 us -> 83.4 us  [the longest x1 54.2 us: body(): psum(psum((sum_first_gain, sum_first_shift, sum_query_bias, sum_value_bia...]
    unnamed x238 -> x236, local copies, waits for them, and re-layouts: 60.9 us -> 60.9 us
  transfers between devices with their start and end apart: 17 -> 18, of which waited for: 9 -> 10; matrix products, arithmetic and copies ran while one was open for 18% -> 19% of each run, Pallas kernels for 0% -> 0%
where the time goes in v1:
time: 1420 us; the launch traced here: 1410 us
  waiting for transfers between devices  559 us (39%)
  other arithmetic  441 us (31%)
  local copies, waits for them, and re-layouts  258 us (18%)
  matrix products  83.5 us (6%)
  blocking collectives  46.6 us (3%)
  between operations  16.1 us (1%)
    scatter-add x2, other arithmetic, body(): sum_table_heads.at[:, flat_index].add(dlogits.reshape(heads, rows * rows))  415 us
    gather x4, local copies, waits for them, and re-layouts, body(): bias = table_by_head[:, position_index]  146 us
    reduce_scatter x1, waiting for transfers between devices, body(): lax.psum_scatter(sum_inner, ('dp', 'mlp'), scatter_dimension=0, tiled=True)  125 us
    reduce_scatter x1, waiting for transfers between devices, body(): lax.psum_scatter(sum_outer, ('dp', 'mlp'), scatter_dimension=0, tiled=True)  103 us
    reduce_scatter x1, waiting for transfers between devices, body(): lax.psum_scatter(sum_down, 'dp', scatter_dimension=1, tiled=True)  72.6 us
    reduce_scatter x1, waiting for transfers between devices, body(): lax.psum_scatter(sum_up, 'dp', scatter_dimension=0, tiled=True)  72.4 us
    unnamed x236, local copies, waits for them, and re-layouts  60.9 us
    psum x1, waiting for transfers between devices, body(): psum(psum((sum_first_gain, sum_first_shift, sum_query_bias, sum_value_bia...  54.2 us
  transfers between devices with their start and end apart: 18, of which 10 were waited for; matrix products, arithmetic and copies ran while one was open for 19% of the time, Pallas kernels for 0%

profile of v1, /device:TPU:0, one launch (start us, length us, event | category | flops | bytes accessed | tf_op | source)
XLA Modules:
  0.0 1414.2 jit_solution(4817378885646267253)
XLA Ops:
  8.7 2.4 fusion.121
  14.8 129.6 %gather_fusion = f32[38809,12]{1,0:T(8,128)} fusion(f32[12,732]{0,1:T(8,128)S(1)} %bitcast.219, s32[38912]{0:T(1024)S(1)} %pad_clamp_fusion), kind=kCustom, calls=%fused_computation | custom fusion | bytes 3880900 | tf_op jit(solution)/shard_map/gather | solution.py:98
  144.5 11.1 copy.105
  155.5 2.8 reshape.322
  158.3 2.3 copy.106
  161.2 3.3 fusion.5
  165.4 1.9 copy.109
  169.2 1.9 copy.111
  171.1 3.0 fusion.4
  177.1 2.0 copy.103
  187.4 1.9 convolution_add_fusion.6
  200.1 2.7 reshape.350
  202.8 2.7 reshape.348
  205.6 7.8 all-gather.23.cloned.1.call-done
  213.4 2.6 reshape.346
  216.1 16.5 %all-gather.21.cloned.1.call-done = bf16[4,197,768]{2,1,0:T(8,128)(2,1)} async-done(((bf16[1,197,768]{2,1,0:T(8,128)(2,1)}), bf16[4,197,768]{2,1,0:T(8,128)(2,1)}) %all-gather.21.cloned.1.call-update) | async-done | bytes 1210384 | tf_op jit(solution)/shard_map/all_gather | solution.py:149
  232.6 2.7 reshape.344
  235.3 40.6 %all-gather.17.cloned.1.call-done = bf16[768,768]{1,0:T(8,128)(2,1)} async-done(((bf16[96,768]{1,0:T(8,128)(2,1)}), bf16[768,768]{1,0:T(8,128)(2,1)}) %all-gather.17.cloned.1.call-update) | async-done | bytes 1179664 | tf_op jit(solution)/shard_map/all_gather | solution.py:43
  275.9 2.9 fusion.125
  280.3 3.5 multiply_convert_fusion.1
  283.8 34.1 %all-gather.19.cloned.1.call-done = bf16[768,768]{0,1:T(8,128)(2,1)} async-done(((bf16[768,96]{0,1:T(8,128)(2,1)}), bf16[768,768]{0,1:T(8,128)(2,1)}) %all-gather.19.cloned.1.call-update) | async-done | bytes 1179664 | tf_op jit(solution)/shard_map/all_gather | solution.py:44
  317.9 4.0 convolution_convert_fusion.2
  322.0 2.3 convolution_convert_fusion.3
  324.3 2.2 convert_reduce_fusion
  326.6 2.2 convolution_convert_fusion
  329.5 2.2 convert_reduce_fusion.1
  332.7 2.2 convolution_convert_fusion.1
  335.0 46.6 %fusion.114 = (bf16[200,768]{1,0:T(8,128)(2,1)}, bf16[200,768]{1,0:T(8,128)(2,1)}, bf16[200,768]{1,0:T(8,128)(2,1)}, bf16[200,768]{1,0:T(8,128)(2,1)}) fusion(bf16[788,768]{1,0:T(8,128)(2,1)} %convolution_convert_fusion.2, bf16[788,768]{1,0:T(8,128)(2,1)} %convolution_convert_fusion.3, bf16[788,768]{1,0:T(8,128)(2,1)} %convolution_convert_fusion, ...), kind=kCustom, calls=%all-reduce-scatter.4 | all-reduce-scatter fusion | flops 2457601 | bytes 6070784
  382.4 1.9 collective-permute-start.2
  385.0 3.2 collective-permute-start.1
  389.0 1.9 collective-permute-start.3
  391.6 1.9 collective-permute-start
  394.1 4.0 concatenate.17
  400.8 4.0 concatenate.16
  404.8 4.0 concatenate.15
  408.8 3.4 fusion.82
  414.3 1.9 copy.119
  416.2 3.2 convolution_convert_fusion.4
  423.9 4.0 concatenate.14
  427.9 3.0 multiply_reduce_fusion.3
  440.0 3.4 copy.123
  443.5 2.2 copy.125
  448.0 4.7 fusion.74
  453.2 2.8 reshape.326
  455.9 9.9 copy.124
  465.8 2.8 reshape.334
  468.6 9.7 copy.126
  478.3 3.8 fusion.90
  489.3 207.4 %scatter_custom_fusion = f32[12,732]{0,1:T(8,128)S(1)} fusion(s32[38809]{0:T(1024)S(1)} %bitcast.254, f32[38809,12]{1,0:T(8,128)} %copy.124, f32[]{:T(128)} %constant.17.clone.1), kind=kCustom, calls=%fused_computation.189 | custom fusion | flops 465708 | bytes 35648 | tf_op jit(solution)/shard_map/scatter-add | solution.py:204
  696.7 207.6 %scatter_fusion = f32[12,732]{0,1:T(8,128)S(1)} fusion(f32[12,732]{0,1:T(8,128)S(1)} %scatter_custom_fusion, s32[38809]{0:T(1024)S(1)} %bitcast.255, f32[38809,12]{1,0:T(8,128)} %copy.126), kind=kCustom, calls=%fused_computation.2 | custom fusion | flops 465708 | bytes 5743732 | tf_op jit(solution)/shard_map/scatter-add | solution.py:204
  905.1 2.0 fusion.105
  907.1 29.2 %all-reduce.16.cloned.1.call-done = (f32[768]{0:T(1024)}, f32[768]{0:T(1024)}, f32[768]{0:T(1024)}, f32[768]{0:T(1024)}, f32[768]{0:T(1024)}, /*index=5*/f32[768...) async-done(((f32[768]{0:T(1024)}, f32[768]{0:T(1024)}, f32[768]{0:T(1024)}, ...) | async-done | bytes 78160 | tf_op jit(solution)/shard_map/psum | solution.py:241
  936.3 3.6 convolution_add_fusion.3
  940.1 3.2 fusion.126
  943.3 2.9 convolution_add_fusion.5
  946.6 3.2 fusion.127
  949.8 2.9 convolution_add_fusion.4
  953.8 2.4 fusion.91
  956.2 4.3 convolution_add_fusion
  964.5 54.2 %all-reduce.14.cloned.1.call-done = (f32[768]{0:T(1024)}, f32[768]{0:T(1024)}, f32[768]{0:T(1024)}, f32[768]{0:T(1024)}, f32[768]{0:T(1024)}, /*index=5*/f32[768...) async-done(((f32[768]{0:T(1024)}, f32[768]{0:T(1024)}, f32[768]{0:T(1024)}, ...) | async-done | bytes 78160 | tf_op jit(solution)/shard_map/psum | solution.py:240
  1020.5 102.6 %reduce-scatter.15.cloned.1.call-done = f32[24,768]{1,0:T(8,128)} async-done(((f32[768,768]{1,0:T(8,128)}), f32[24,768]{1,0:T(8,128)}) %reduce-scatter.15.cloned.1.call-update) | async-done | bytes 73744 | tf_op jit(solution)/shard_map/reduce_scatter | solution.py:231
  1123.1 72.4 %reduce-scatter.17.cloned.1.call-done = f32[96,768]{1,0:T(8,128)} async-done(((f32[768,768]{1,0:T(8,128)}), f32[96,768]{1,0:T(8,128)}) %reduce-scatter.17.cloned.1.call-update) | async-done | bytes 294928 | tf_op jit(solution)/shard_map/reduce_scatter | solution.py:234
  1195.5 72.6 %reduce-scatter.19.cloned.1.call-done = f32[768,96]{0,1:T(8,128)} async-done(((f32[768,768]{0,1:T(8,128)}), f32[768,96]{0,1:T(8,128)}) %reduce-scatter.19.cloned.1.call-update) | async-done | bytes 294928 | tf_op jit(solution)/shard_map/reduce_scatter | solution.py:235
  1268.2 125.3 %reduce-scatter.13.cloned.1.call-done = f32[24,2304]{1,0:T(8,128)} async-done(((f32[768,2304]{1,0:T(8,128)}), f32[24,2304]{1,0:T(8,128)}) %reduce-scatter.13.cloned.1.call-update) | async-done | bytes 221200 | tf_op jit(solution)/shard_map/reduce_scatter | solution.py:230
  (345 shorter events, 86.3 us)
Async XLA Ops:
  7.2 3.9 copy-start.69
  7.2 153.9 %all-gather.13.cloned.1.call-start = ((), (), s32[]{:S(2)}) async-start(), calls=%async_computation.4 | async-start | bytes 3649536 | tf_op jit(solution)/shard_map/all_gather | solution.py:39
  7.9 179.4 %all-gather.15.cloned.1.call-start = ((), (), s32[]{:S(2)}) async-start(), calls=%async_computation.5 | async-start | bytes 1216512 | tf_op jit(solution)/shard_map/all_gather | solution.py:40
  8.7 4.2 copy-start.35
  8.7 191.4 %all-gather.27.cloned.1.call-start = ((), (), s32[]{:S(2)}) async-start(), calls=%async_computation.15 | async-start | bytes 1536000 | tf_op jit(solution)/shard_map/all_gather | solution.py:170
  12.3 190.5 %all-gather.25.cloned.1.call-start = ((), (), s32[]{:S(2)}) async-start(), calls=%async_computation.14 | async-start | bytes 1536000 | tf_op jit(solution)/shard_map/all_gather | solution.py:170
  12.9 200.5 %all-gather.23.cloned.1.call-start = ((), (), s32[]{:S(2)}) async-start(), calls=%async_computation.13 | async-start | bytes 1536000 | tf_op jit(solution)/shard_map/all_gather | solution.py:149
  14.0 157.2 %copy-start.16 = (bf16[1,197,768]{2,1,0:T(8,128)(2,1)}, bf16[1,197,768]{2,1,0:T(8,128)(2,1)S(1)}, u32[]{:S(2)}) copy-start(bf16[1,197,768]{2,1,0:T(8,128)(2,1)S(1)} %get-tuple-element.191) | copy-start | bytes 907780
  14.2 146.9 %copy-start.71 = (f32[197]{0:T(256)}, f32[197]{0:T(256)S(1)}, u32[]{:S(2)}) copy-start(f32[197]{0:T(256)S(1)} %add_rsqrt_fusion.1) | copy-start | bytes 2368
  160.6 18.5 %copy-start.6 = (f32[197,197,12]{0,1,2:T(8,128)}, f32[197,197,12]{0,1,2:T(8,128)S(1)}, u32[]{:S(2)}) copy-start(f32[197,197,12]{0,1,2:T(8,128)S(1)} %copy.106) | copy-start | bytes 5588500
  160.7 10.5 copy-start.77
  160.9 10.2 copy-start.87
  177.1 6.6 copy-start.23
  190.8 4.0 copy-start.73
  191.1 3.8 copy-start.75
  191.3 3.6 copy-start.82
  192.8 39.8 %all-gather.21.cloned.1.call-start = ((), (), s32[]{:S(2)}) async-start(), calls=%async_computation.12 | async-start | bytes 1536000 | tf_op jit(solution)/shard_map/all_gather | solution.py:149
  193.3 82.5 %all-gather.17.cloned.1.call-start = ((), (), s32[]{:S(2)}) async-start(), calls=%async_computation.6 | async-start | bytes 1327104 | tf_op jit(solution)/shard_map/all_gather | solution.py:43
  194.1 123.8 %all-gather.19.cloned.1.call-start = ((), (), s32[]{:S(2)}) async-start(), calls=%async_computation.7 | async-start | bytes 1327104 | tf_op jit(solution)/shard_map/all_gather | solution.py:44
  194.9 741.4 %all-reduce.16.cloned.1.call-start = ((), (), s32[]{:S(2)}) async-start(), calls=%async_computation.17 | async-start | bytes 860160 | tf_op jit(solution)/shard_map/psum | solution.py:241
  200.0 5.5 copy-start.59
  200.1 5.5 copy-start.63
  200.1 5.5 copy-start.61
  200.1 5.5 copy-start.65
  275.9 4.4 copy-start.51
  275.9 4.4 copy-start.93
  317.9 4.0 copy-start.95
  317.9 4.0 copy-start.100
  334.9 63.1 %copy-start.76 = (f32[197]{0:T(256)S(1)}, f32[197]{0:T(256)}, u32[]{:S(2)}) copy-start(f32[197]{0:T(256)} %copy-done.75) | copy-start | bytes 2368
  335.0 63.1 %copy-start.86 = (f32[197]{0:T(256)S(1)}, f32[197]{0:T(256)}, u32[]{:S(2)}) copy-start(f32[197]{0:T(256)} %copy-done.85) | copy-start | bytes 2368
  381.5 27.2 %copy-start.70 = (f32[768]{0:T(1024)S(1)}, f32[768]{0:T(1024)}, u32[]{:S(2)}) copy-start(f32[768]{0:T(1024)} %param.38) | copy-start | bytes 9220
  381.6 27.2 %copy-start.74 = (f32[197]{0:T(256)S(1)}, f32[197]{0:T(256)}, u32[]{:S(2)}) copy-start(f32[197]{0:T(256)} %copy-done.73) | copy-start | bytes 2368
  381.6 27.2 %copy-start.80 = (f32[768]{0:T(1024)S(1)}, f32[768]{0:T(1024)}, u32[]{:S(2)}) copy-start(f32[768]{0:T(1024)} %param.37) | copy-start | bytes 9220
  381.6 27.2 %copy-start.83 = (f32[197]{0:T(256)S(1)}, f32[197]{0:T(256)}, u32[]{:S(2)}) copy-start(f32[197]{0:T(256)} %copy-done.82) | copy-start | bytes 2368
  382.4 18.4 %collective-permute-start.2 = (bf16[9,768]{1,0:T(8,128)(2,1)S(1)}, bf16[9,768]{1,0:T(8,128)(2,1)}, u32[]{:S(2)}, u32[]{:S(2)}) collective-permute-start(bf16[9,768]{1,0:T(8,128)(2,1)S(1)} %slice.62), channel_id=1, source_target_pairs={{0,1},{1,2},{2,3},{4,5},{5,6},{6,7},{8,9},{9,10},{10,11},{12,13},{... | collective-permute-start | bytes 41480
  385.0 19.8 %collective-permute-start.1 = (bf16[9,768]{1,0:T(8,128)(2,1)S(1)}, bf16[9,768]{1,0:T(8,128)(2,1)}, u32[]{:S(2)}, u32[]{:S(2)}) collective-permute-start(bf16[9,768]{1,0:T(8,128)(2,1)S(1)} %slice.61), channel_id=1, source_target_pairs={{0,1},{1,2},{2,3},{4,5},{5,6},{6,7},{8,9},{9,10},{10,11},{12,13},{... | collective-permute-start | bytes 41480
  389.0 5.1 collective-permute-start.3
  391.6 32.3 %collective-permute-start = (bf16[9,768]{1,0:T(8,128)(2,1)S(1)}, bf16[9,768]{1,0:T(8,128)(2,1)}, u32[]{:S(2)}, u32[]{:S(2)}) collective-permute-start(bf16[9,768]{1,0:T(8,128)(2,1)S(1)} %slice.60), channel_id=1, source_target_pairs={{0,1},{1,2},{2,3},{4,5},{5,6},{6,7},{8,9},{9,10},{10,11},{12,13},{... | collective-permute-start | bytes 41480
  394.0 18.2 %copy-start.68 = (f32[3072]{0:T(1024)}, f32[3072]{0:T(1024)S(1)}, u32[]{:S(2)}) copy-start(f32[3072]{0:T(1024)S(1)} %add_dynamic-update-slice_fusion) | copy-start | bytes 36868
  408.8 4.3 copy-start.9
  422.7 5.2 copy-start.81
  422.7 5.2 copy-start.84
  427.9 3.9 copy-start.10
  440.0 3.4 copy-start.4
  443.4 4.6 copy-start.18
  443.4 4.6 copy-start.78
  443.5 4.6 copy-start.88
  448.0 4.8 copy-start.31
  448.0 4.9 copy-start.29
  478.3 3.8 copy-start.13
  478.3 3.8 copy-start.54
  478.3 3.8 copy-start.72
  482.0 214.7 %copy-start.33 = (f32[197,768]{1,0:T(8,128)}, f32[197,768]{1,0:T(8,128)S(1)}, u32[]{:S(2)}) copy-start(f32[197,768]{1,0:T(8,128)S(1)} %fusion.90) | copy-start | bytes 1815556
  482.0 7.2 copy-start.53
  696.7 208.4 %copy-start.37 = (bf16[12,64,197]{2,1,0:T(8,128)(2,1)S(1)}, bf16[12,64,197]{2,1,0:T(8,128)(2,1)}, u32[]{:S(2)}) copy-start(bf16[12,64,197]{2,1,0:T(8,128)(2,1)} %convolution_convert_fusion.7) | copy-start | bytes 907780
  904.3 32.0 %copy-start.15 = (f32[197,768]{1,0:T(8,128)S(1)}, f32[197,768]{1,0:T(8,128)}, u32[]{:S(2)}) copy-start(f32[197,768]{1,0:T(8,128)} %copy-done.14) | copy-start | bytes 1815556
  904.3 32.0 %copy-start.42 = (bf16[12,64,197]{2,1,0:T(8,128)(2,1)S(1)}, bf16[12,64,197]{2,1,0:T(8,128)(2,1)}, u32[]{:S(2)}) copy-start(bf16[12,64,197]{2,1,0:T(8,128)(2,1)} %convolution_convert_fusion.6) | copy-start | bytes 907780
  905.1 113.6 %all-reduce.14.cloned.1.call-start = ((), (), s32[]{:S(2)}) async-start(), calls=%async_computation.16 | async-start | bytes 860160 | tf_op jit(solution)/shard_map/psum | solution.py:240
  936.3 186.8 %reduce-scatter.15.cloned.1.call-start = ((), (), s32[]{:S(2)}) async-start(), calls=%async_computation.9 | async-start | bytes 2433024 | tf_op jit(solution)/shard_map/reduce_scatter | solution.py:231
  940.0 255.5 %reduce-scatter.17.cloned.1.call-start = ((), (), s32[]{:S(2)}) async-start(), calls=%async_computation.10 | async-start | bytes 2654208 | tf_op jit(solution)/shard_map/reduce_scatter | solution.py:234
  946.3 321.9 %reduce-scatter.19.cloned.1.call-start = ((), (), s32[]{:S(2)}) async-start(), calls=%async_computation.11 | async-start | bytes 2654208 | tf_op jit(solution)/shard_map/reduce_scatter | solution.py:235
  952.7 3.5 copy-start.30
  952.7 3.5 copy-start.32
  952.7 440.7 %reduce-scatter.13.cloned.1.call-start = ((), (), s32[]{:S(2)}) async-start(), calls=%async_computation.8 | async-start | bytes 7299072 | tf_op jit(solution)/shard_map/reduce_scatter | solution.py:230
  (58 other events, 119.9 us)
Sparse Core Ops, SparseCore 0:
  10.9 62.8 all-gather.12
  76.7 52.8 all-gather.14
  131.2 16.6 all-gather.26
  149.3 17.7 all-gather.24
  192.9 20.4 all-gather.22
  214.8 17.7 all-gather.20
  234.8 41.0 all-gather.16
  278.1 39.8 all-gather.18
  905.2 31.0 all-reduce.15
  941.9 76.7 all-reduce.13
  1024.6 98.4 reduce-scatter.14
  1127.4 68.0 reduce-scatter.16
  1200.0 68.0 reduce-scatter.18
  1275.2 118.2 reduce-scatter.12
